TPU v7x, 512 devices: a whole 4x4x16 slice. The times are simulated.
512 devices in a mesh: ctx: 64 (over z, x), head: 8 (over y, core).
Axes of the slice: x: 4, y: 4, z: 16, core: 2. Of those that a mesh axis runs over, the one named last changes fastest.
Arguments:
- queries: bfloat16 [16384, 32, 576], P('ctx', 'head'), may hold values from -1024 to 1024
- latent_kv: bfloat16 [16384, 576], P('ctx'), may hold values from -6 to 6
- out_grad: bfloat16 [16384, 32, 512], P('ctx', 'head'), may hold values from -6 to 6
- lengths: int32 [32], replicated, may hold values from 1 to 1024, as said below
- block_plan: int32 [128], replicated, may hold values from 0 to 63, as said below
Outputs:
- query_grad: bfloat16 [16384, 32, 576], P('ctx', 'head')
- latent_grad: float32 [16384, 576], P(('ctx', 'head'))
Inputs may be any that keep to these rules, and one draw needn't show every extreme that they name: `lengths`: 32 documents laid end to end; they sum to 16384, and one has exactly 1024 tokens. `block_plan`: block b is held by device b // 2, except that the last block of a device may trade places with the last block of the device 64 // 2 indices away on ctx; trades are mutual, and the last device on ctx always trades.
All inputs are finite; a program needn't handle non-finite values.
Results may differ from a plain program's by a relative error of at most 0.0049.
Values may be sent and summed in bfloat16 or wider, within the bound.
A program may use at most 128 MiB of HBM per device.

v0:
```python
import jax
import jax.numpy as jnp
from jax import lax
from jax.sharding import PartitionSpec as P

BLOCK = 128
MOST = 1024


SCORE_SCALE = 192.0 ** (-0.5)
MASKED_FILL = -1e30


def from_behind(value, axis, by):
    peers = lax.axis_size(axis)
    pairs = [(i, i + by) for i in range(peers) if 0 <= i + by < peers]
    return lax.ppermute(value, axis, pairs)


def passed_along(value, axis, by):
    peers = lax.axis_size(axis)
    return lax.ppermute(value, axis, [(i, (i + by) % peers) for i in range(peers)])


def doc_index(positions, doc_ends):
    inside = jnp.sum((doc_ends[None, :] <= positions[:, None]).astype(jnp.int32), axis=1)
    return jnp.where(positions < 0, -1, inside)


def block_grads(query_block, grad_block, window, query_start, window_start, doc_ends, doc_starts):
    block_rows, head_count, column_count = query_block.shape
    latent = grad_block.shape[2]
    row_count = block_rows * head_count
    tile_count = window.shape[0] // block_rows
    query_rows = query_block.reshape(row_count, column_count)
    grad_rows = grad_block.reshape(row_count, latent)
    query_pos = query_start + jnp.arange(block_rows, dtype=jnp.int32)
    query_docs = doc_index(query_pos, doc_ends)
    doc_begin = jnp.sum(
        jnp.where(jnp.arange(doc_ends.shape[0], dtype=jnp.int32) == query_docs[0], doc_starts, 0)
    )
    first_tile = jnp.maximum((doc_begin - window_start) // block_rows, 0)
    end_tile = (query_start - window_start) // block_rows + 1

    def first_pass(tile_index, state_now):
        scores_all, grads_all, row_top, row_total, weighted = state_now
        key_tile = lax.dynamic_slice_in_dim(window, tile_index * block_rows, block_rows, 0)
        key_pos = window_start + tile_index * block_rows + jnp.arange(block_rows, dtype=jnp.int32)
        allowed = (doc_index(key_pos, doc_ends)[None, :] == query_docs[:, None]) & (
            key_pos[None, :] <= query_pos[:, None]
        )
        scores = jnp.einsum("rc,kc->rk", query_rows, key_tile, preferred_element_type=jnp.float32)
        scores = scores.reshape(block_rows, head_count, block_rows) * SCORE_SCALE
        scores = jnp.where(allowed[:, None, :], scores, MASKED_FILL)
        values_grad = jnp.einsum(
            "rl,kl->rk", grad_rows, key_tile[:, :latent], preferred_element_type=jnp.float32
        )
        values_grad = values_grad.reshape(block_rows, head_count, block_rows)
        new_top = jnp.maximum(row_top, jnp.max(scores, axis=2))
        rescale = jnp.exp(row_top - new_top)
        weights = jnp.exp(scores - new_top[:, :, None])
        row_total = row_total * rescale + jnp.sum(weights, axis=2)
        weighted = weighted * rescale + jnp.sum(weights * values_grad, axis=2)
        scores_all = lax.dynamic_update_index_in_dim(scores_all, scores, tile_index, 0)
        grads_all = lax.dynamic_update_index_in_dim(grads_all, values_grad, tile_index, 0)
        return (scores_all, grads_all, new_top, row_total, weighted)

    buffer_zero = jnp.zeros((tile_count, block_rows, head_count, block_rows), jnp.float32)
    stat_zero = jnp.zeros((block_rows, head_count), jnp.float32)
    start_state = (
        buffer_zero,
        buffer_zero,
        jnp.full((block_rows, head_count), MASKED_FILL, jnp.float32),
        stat_zero,
        stat_zero,
    )
    scores_all, grads_all, row_top, row_total, weighted = lax.fori_loop(
        first_tile, end_tile, first_pass, start_state
    )
    delta = weighted / row_total

    def second_pass(tile_index, state_now):
        query_grad, window_grad = state_now
        key_tile = lax.dynamic_slice_in_dim(window, tile_index * block_rows, block_rows, 0)
        scores = lax.dynamic_index_in_dim(scores_all, tile_index, 0, keepdims=False)
        values_grad = lax.dynamic_index_in_dim(grads_all, tile_index, 0, keepdims=False)
        probability = jnp.exp(scores - row_top[:, :, None]) / row_total[:, :, None]
        score_grad = (
            (probability * (values_grad - delta[:, :, None]))
            .astype(jnp.bfloat16)
            .reshape(row_count, block_rows)
        )
        probs_low = probability.astype(jnp.bfloat16).reshape(row_count, block_rows)
        query_grad = query_grad + SCORE_SCALE * jnp.einsum(
            "rk,kc->rc", score_grad, key_tile, preferred_element_type=jnp.float32
        )
        key_part = SCORE_SCALE * jnp.einsum(
            "rk,rc->kc", score_grad, query_rows, preferred_element_type=jnp.float32
        )
        value_part = jnp.einsum(
            "rk,rl->kl", probs_low, grad_rows, preferred_element_type=jnp.float32
        )
        tile_grad = key_part + jnp.pad(value_part, ((0, 0), (0, column_count - latent)))
        current = lax.dynamic_slice_in_dim(window_grad, tile_index * block_rows, block_rows, 0)
        window_grad = lax.dynamic_update_slice_in_dim(
            window_grad, current + tile_grad, tile_index * block_rows, 0
        )
        return (query_grad, window_grad)

    grad_start = (
        jnp.zeros((row_count, column_count), jnp.float32),
        jnp.zeros(window.shape, jnp.float32),
    )
    query_grad, window_grad = lax.fori_loop(first_tile, end_tile, second_pass, grad_start)
    return (query_grad.reshape(block_rows, head_count, column_count), window_grad)


def local_blocks(
    query_blocks, grad_blocks, block_total, window, shard_start, window_start, doc_ends, doc_starts
):

    def advance(window_grad, inputs):
        block_number, query_block, grad_block = inputs
        query_grad, window_part = block_grads(
            query_block,
            grad_block,
            window,
            shard_start + block_number * BLOCK,
            window_start,
            doc_ends,
            doc_starts,
        )
        return (window_grad + window_part, query_grad.astype(jnp.bfloat16))

    inputs = (jnp.arange(block_total, dtype=jnp.int32), query_blocks, grad_blocks)
    return lax.scan(advance, jnp.zeros(window.shape, jnp.float32), inputs)


def on_device(queries, latent_kv, out_grad, lengths, block_plan):
    tok_rows, head_count, column_count = queries.shape
    latent = out_grad.shape[2]
    blocks_here = tok_rows // BLOCK
    reach = (MOST + tok_rows - 2) // tok_rows
    ctx_count = lax.axis_size("ctx")
    position = lax.axis_index("ctx")
    doc_ends = jnp.cumsum(lengths)
    doc_starts = doc_ends - lengths
    earlier = []
    for hop_count in range(reach, 0, -1):
        earlier.append(from_behind(latent_kv, "ctx", hop_count))
    window = jnp.concatenate(earlier + [latent_kv], axis=0)
    window_start = (position - reach) * tok_rows
    shard_start = position * tok_rows
    query_blocks = queries.reshape(blocks_here, BLOCK, head_count, column_count)
    grad_blocks = out_grad.reshape(blocks_here, BLOCK, head_count, latent)
    half_axis = ctx_count // 2
    last_block = position * blocks_here + blocks_here - 1
    holder = jnp.sum(
        jnp.where(jnp.arange(block_plan.shape[0], dtype=jnp.int32) == last_block, block_plan, 0)
    )
    traded = holder != position
    window_grad, query_parts = local_blocks(
        query_blocks,
        grad_blocks,
        blocks_here,
        window,
        shard_start,
        window_start,
        doc_ends,
        doc_starts,
    )
    last_grad = query_parts[blocks_here - 1]
    received = passed_along(last_grad, "ctx", half_axis)
    last_out = jnp.where(traded, received, last_grad)
    query_out = jnp.concatenate([query_parts[: blocks_here - 1], last_out[None]], axis=0)
    query_grad = query_out.reshape(tok_rows, head_count, column_count)
    shares = window_grad.reshape(reach + 1, tok_rows, column_count)
    gathered = shares[reach]
    for hop_count in range(1, reach + 1):
        gathered = gathered + from_behind(
            shares[reach - hop_count].astype(jnp.bfloat16), "ctx", -hop_count
        ).astype(jnp.float32)
    latent_grad = lax.psum_scatter(gathered, "head", scatter_dimension=0, tiled=True)
    return (query_grad, latent_grad)


def solution(mesh):
    return jax.shard_map(
        on_device,
        mesh=mesh,
        in_specs=(P("ctx", "head", None), P("ctx", None), P("ctx", "head", None), P(), P()),
        out_specs=(P("ctx", "head", None), P(("ctx", "head"), None)),
        check_vma=False,
    )
```

profile of v0, /device:TPU:1, one launch (start us, length us, event | category | flops | bytes accessed | tf_op | source)
XLA Modules:
  0.0 366.3 jit_solution(1400249240749378241)
XLA Ops:
  8.4 4.4 %collective-permute-start = (bf16[256,576]{1,0:T(8,128)(2,1)S(1)}, bf16[256,576]{1,0:T(8,128)(2,1)S(1)}, u32[]{:S(2)}, u32[]{:S(2)}) collective-permute-start(bf16[256,576]{1,0:T(8,128)(2,1)S(1)} %copy.75), channel_id=1, source_target_pairs={{0,32},{8,40},{16,48},{24,56},{32,64},{40,72},{48,80},{56,88},{64,... | collective-permute-start | bytes 884744 | tf_op jit(solution)/shard_map/ppermute | solution.py:17
  12.8 4.4 %collective-permute-start.1 = (bf16[256,576]{1,0:T(8,128)(2,1)S(1)}, bf16[256,576]{1,0:T(8,128)(2,1)S(1)}, u32[]{:S(2)}, u32[]{:S(2)}) collective-permute-start(bf16[256,576]{1,0:T(8,128)(2,1)S(1)} %copy.75), channel_id=1, source_target_pairs={{0,24},{8,32},{16,40},{24,48},{32,56},{40,64},{48,72},{56,80},{64,... | collective-permute-start | bytes 884744 | tf_op jit(solution)/shard_map/ppermute | solution.py:17
  17.2 3.8 %collective-permute-start.2 = (bf16[256,576]{1,0:T(8,128)(2,1)S(1)}, bf16[256,576]{1,0:T(8,128)(2,1)S(1)}, u32[]{:S(2)}, u32[]{:S(2)}) collective-permute-start(bf16[256,576]{1,0:T(8,128)(2,1)S(1)} %copy.75), channel_id=1, source_target_pairs={{0,16},{8,24},{16,32},{24,40},{32,48},{40,56},{48,64},{56,72},{64,... | collective-permute-start | bytes 884744 | tf_op jit(solution)/shard_map/ppermute | solution.py:17
  21.0 2.5 collective-permute-start.3
  25.1 3.4 copy.74
  30.2 3.6 collective-permute-done.3
  35.0 73.5 %while.83 = (s32[]{:T(128)}, f32[1280,576]{0,1:T(8,128)}, bf16[2,128,4,576]{1,3,2,0:T(8,128)(2,1)}, s32[2]{0:T(128)S(1)}, s32[]{:T(128)}, /*index=5*/s32[32]{0:T...) while((s32[]{:T(128)}, f32[1280,576]{0,1:T(8,128)}, ...), condition=%wide.region_12.13_spmd.clone, body=%wide.region_1.12_spmd.clone.sunk | while | flops 364809216 | bytes 52867096 | solution.py:136
  40.9 2.0 broadcast.218
  42.9 2.0 broadcast.218.clone
  44.9 4.7 %while.84 = (s32[]{:T(128)}, f32[10,128,4,128]{3,2,1,0:T(4,128)}, f32[10,128,4,128]{3,2,1,0:T(4,128)}, f32[128,4]{1,0:T(8,128)S(1)}, f32[128,4]{1,0:T(8,128)S(1)...) while((s32[]{:T(128)}, f32[10,128,4,128]{3,2,1,0:T(4,128)}, ...), condition=%wide.region_9.9_spmd.clone, body=%wide.region_4.8_spmd.clone.sunk | while | flops 143259648 | bytes 4726177 | solution.py:77
  50.1 1.8 broadcast.217
  52.1 5.6 %while.85 = (s32[]{:T(128)}, f32[512,576]{0,1:T(8,128)S(1)}, f32[1280,576]{0,1:T(8,128)}, s32[]{:T(128)}, f32[10,128,4,128]{3,2,1,0:T(4,128)}, /*index=5*/f32[12...) while((s32[]{:T(128)}, f32[512,576]{0,1:T(8,128)S(1)}, ...), condition=%wide.wide.region_11.11_spmd, body=%wide.wide.region_10.10_spmd.sunk | while | flops 219766784 | bytes 7127313 | solution.py:114
  53.7 2.3 fusion.56
  58.8 2.4 convert_element_type.94
  63.7 2.0 select_add_fusion.2
  71.5 2.0 broadcast.218
  73.5 2.0 broadcast.218.clone
  75.6 9.5 %while.84 = (s32[]{:T(128)}, f32[10,128,4,128]{3,2,1,0:T(4,128)}, f32[10,128,4,128]{3,2,1,0:T(4,128)}, f32[128,4]{1,0:T(8,128)S(1)}, f32[128,4]{1,0:T(8,128)S(1)...) while((s32[]{:T(128)}, f32[10,128,4,128]{3,2,1,0:T(4,128)}, ...), condition=%wide.region_9.9_spmd.clone, body=%wide.region_4.8_spmd.clone.sunk | while | flops 143259648 | bytes 4726177 | solution.py:77
  85.5 1.8 broadcast.217
  87.5 11.2 %while.85 = (s32[]{:T(128)}, f32[512,576]{0,1:T(8,128)S(1)}, f32[1280,576]{0,1:T(8,128)}, s32[]{:T(128)}, f32[10,128,4,128]{3,2,1,0:T(4,128)}, /*index=5*/f32[12...) while((s32[]{:T(128)}, f32[512,576]{0,1:T(8,128)S(1)}, ...), condition=%wide.wide.region_11.11_spmd, body=%wide.wide.region_10.10_spmd.sunk | while | flops 219766784 | bytes 7127313 | solution.py:114
  89.1 2.3 fusion.56
  94.7 2.4 fusion.56
  99.8 2.4 convert_element_type.94
  104.7 3.8 %select_add_fusion.2 = f32[1280,576]{0,1:T(8,128)} fusion(f32[1280,576]{0,1:T(8,128)S(1)} %copy-done, f32[1280,576]{0,1:T(8,128)} %get-tuple-element.1155, pred[]{:T(512)S(6)} %compare.18), kind=kLoop, calls=%fused_computation.37.clone.1 | loop fusion | flops 1474560 | bytes 8847361 | tf_op jit(solution)/shard_map/while/body/eval_jaxpr/add | solution.py:133
  108.5 2.4 copy.83
  116.4 26.6 %collective-permute-done.5 = bf16[256,576]{1,0:T(8,128)(2,1)S(1)} collective-permute-done((bf16[256,576]{1,0:T(8,128)(2,1)S(1)}, bf16[256,576]{1,0:T(8,128)(2,1)S(1)}, u32[]{:S(2)}, u32[]{:S(2)}) %collective-permute-start.5) | collective-permute-done | bytes 294944 | tf_op jit(solution)/shard_map/ppermute | solution.py:17
  143.0 26.3 %collective-permute-done.6 = bf16[256,576]{1,0:T(8,128)(2,1)S(1)} collective-permute-done((bf16[256,576]{1,0:T(8,128)(2,1)S(1)}, bf16[256,576]{1,0:T(8,128)(2,1)S(1)}, u32[]{:S(2)}, u32[]{:S(2)}) %collective-permute-start.6) | collective-permute-done | bytes 294944 | tf_op jit(solution)/shard_map/ppermute | solution.py:17
  169.3 45.9 %collective-permute-done.7 = bf16[256,576]{1,0:T(8,128)(2,1)S(1)} collective-permute-done((bf16[256,576]{1,0:T(8,128)(2,1)S(1)}, bf16[256,576]{1,0:T(8,128)(2,1)S(1)}, u32[]{:S(2)}, u32[]{:S(2)}) %collective-permute-start.7) | collective-permute-done | bytes 294944 | tf_op jit(solution)/shard_map/ppermute | solution.py:17
  215.2 21.8 %collective-permute-done.8 = bf16[256,576]{1,0:T(8,128)(2,1)S(1)} collective-permute-done((bf16[256,576]{1,0:T(8,128)(2,1)S(1)}, bf16[256,576]{1,0:T(8,128)(2,1)S(1)}, u32[]{:S(2)}, u32[]{:S(2)}) %collective-permute-start.8) | collective-permute-done | bytes 294944 | tf_op jit(solution)/shard_map/ppermute | solution.py:17
  239.4 13.1 %collective-permute-start.4 = (bf16[128,4,576]{0,2,1:T(8,128)(2,1)S(1)}, bf16[128,4,576]{0,2,1:T(8,128)(2,1)S(1)}, u32[]{:S(2)}, u32[]{:S(2)}) collective-permute-start(bf16[128,4,576]{0,2,1:T(8,128)(2,1)S(1)} %get-tuple-element.619), channel_id=1, source_target_pairs={{0,256},{8,264},{16,272},{24,280},{32,288},{40,296},{48,304},{56,3... | collective-permute-start | bytes 1769480 | tf_op jit(solution)/shard_map/ppermute | solution.py:22
  253.8 12.7 %collective-permute-done.4 = bf16[128,4,576]{0,2,1:T(8,128)(2,1)S(1)} collective-permute-done((bf16[128,4,576]{0,2,1:T(8,128)(2,1)S(1)}, bf16[128,4,576]{0,2,1:T(8,128)(2,1)S(1)}, u32[]{:S(2)}, u32[]{:S(2)}) %collective-permute-start.4) | collective-permute-done | bytes 589856 | tf_op jit(solution)/shard_map/ppermute | solution.py:22
  267.8 91.6 %reduce-scatter.2.cloned.1.call-done = f32[32,576]{1,0:T(8,128)} async-done(((f32[256,576]{1,0:T(8,128)}), f32[32,576]{1,0:T(8,128)}) %reduce-scatter.2.cloned.1.call-update) | async-done | bytes 73744 | tf_op jit(solution)/shard_map/reduce_scatter | solution.py:183
  (159 shorter events, 55.8 us)
Async XLA Ops:
  7.2 352.3 %reduce-scatter.2.cloned.1.call-start = ((), (), s32[]{:S(2)}) async-start(), calls=%async_computation.1 | async-start | bytes 737280 | tf_op jit(solution)/shard_map/reduce_scatter | solution.py:183
  8.4 20.1 %collective-permute-start = (bf16[256,576]{1,0:T(8,128)(2,1)S(1)}, bf16[256,576]{1,0:T(8,128)(2,1)S(1)}, u32[]{:S(2)}, u32[]{:S(2)}) collective-permute-start(bf16[256,576]{1,0:T(8,128)(2,1)S(1)} %copy.75), channel_id=1, source_target_pairs={{0,32},{8,40},{16,48},{24,56},{32,64},{40,72},{48,80},{56,88},{64,... | collective-permute-start | bytes 884744 | tf_op jit(solution)/shard_map/ppermute | solution.py:17
  12.8 17.3 %collective-permute-start.1 = (bf16[256,576]{1,0:T(8,128)(2,1)S(1)}, bf16[256,576]{1,0:T(8,128)(2,1)S(1)}, u32[]{:S(2)}, u32[]{:S(2)}) collective-permute-start(bf16[256,576]{1,0:T(8,128)(2,1)S(1)} %copy.75), channel_id=1, source_target_pairs={{0,24},{8,32},{16,40},{24,48},{32,56},{40,64},{48,72},{56,80},{64,... | collective-permute-start | bytes 884744 | tf_op jit(solution)/shard_map/ppermute | solution.py:17
  17.2 12.9 %collective-permute-start.2 = (bf16[256,576]{1,0:T(8,128)(2,1)S(1)}, bf16[256,576]{1,0:T(8,128)(2,1)S(1)}, u32[]{:S(2)}, u32[]{:S(2)}) collective-permute-start(bf16[256,576]{1,0:T(8,128)(2,1)S(1)} %copy.75), channel_id=1, source_target_pairs={{0,16},{8,24},{16,32},{24,40},{32,48},{40,56},{48,64},{56,72},{64,... | collective-permute-start | bytes 884744 | tf_op jit(solution)/shard_map/ppermute | solution.py:17
  21.0 12.8 %collective-permute-start.3 = (bf16[256,576]{1,0:T(8,128)(2,1)S(1)}, bf16[256,576]{1,0:T(8,128)(2,1)S(1)}, u32[]{:S(2)}, u32[]{:S(2)}) collective-permute-start(bf16[256,576]{1,0:T(8,128)(2,1)S(1)} %copy.75), channel_id=1, source_target_pairs={{0,8},{8,16},{16,24},{24,32},{32,40},{40,48},{48,56},{56,64},{64,7... | collective-permute-start | bytes 884744 | tf_op jit(solution)/shard_map/ppermute | solution.py:17
  33.9 1.2 copy-start.3
  49.7 2.2 copy-start.1
  49.7 2.2 copy-start.2
  49.7 2.3 copy-start.4
  58.8 4.9 %copy-start = (f32[1280,576]{0,1:T(8,128)S(1)}, f32[1280,576]{0,1:T(8,128)}, u32[]{:S(2)}) copy-start(f32[1280,576]{0,1:T(8,128)} %get-tuple-element.967) | copy-start | bytes 8847364 | tf_op jit(solution)/shard_map/while
  85.1 2.2 copy-start.1
  85.1 2.2 copy-start.2
  85.1 2.3 copy-start.4
  99.8 4.9 %copy-start = (f32[1280,576]{0,1:T(8,128)S(1)}, f32[1280,576]{0,1:T(8,128)}, u32[]{:S(2)}) copy-start(f32[1280,576]{0,1:T(8,128)} %get-tuple-element.967) | copy-start | bytes 8847364 | tf_op jit(solution)/shard_map/while
  111.2 31.8 %collective-permute-start.5 = (bf16[256,576]{1,0:T(8,128)(2,1)S(1)}, bf16[256,576]{1,0:T(8,128)(2,1)S(1)}, u32[]{:S(2)}, u32[]{:S(2)}) collective-permute-start(bf16[256,576]{1,0:T(8,128)(2,1)S(1)} %get-tuple-element.614), channel_id=1, source_target_pairs={{8,0},{16,8},{24,16},{32,24},{40,32},{48,40},{56,48},{64,56},{72,6... | collective-permute-start | bytes 884744 | tf_op jit(solution)/shard_map/ppermute | solution.py:17
  112.5 56.8 %collective-permute-start.6 = (bf16[256,576]{1,0:T(8,128)(2,1)S(1)}, bf16[256,576]{1,0:T(8,128)(2,1)S(1)}, u32[]{:S(2)}, u32[]{:S(2)}) collective-permute-start(bf16[256,576]{1,0:T(8,128)(2,1)S(1)} %get-tuple-element.617), channel_id=1, source_target_pairs={{16,0},{24,8},{32,16},{40,24},{48,32},{56,40},{64,48},{72,56},{80,... | collective-permute-start | bytes 884744 | tf_op jit(solution)/shard_map/ppermute | solution.py:17
  113.8 101.4 %collective-permute-start.7 = (bf16[256,576]{1,0:T(8,128)(2,1)S(1)}, bf16[256,576]{1,0:T(8,128)(2,1)S(1)}, u32[]{:S(2)}, u32[]{:S(2)}) collective-permute-start(bf16[256,576]{1,0:T(8,128)(2,1)S(1)} %get-tuple-element.616), channel_id=1, source_target_pairs={{24,0},{32,8},{40,16},{48,24},{56,32},{64,40},{72,48},{80,56},{88,... | collective-permute-start | bytes 884744 | tf_op jit(solution)/shard_map/ppermute | solution.py:17
  115.1 121.9 %collective-permute-start.8 = (bf16[256,576]{1,0:T(8,128)(2,1)S(1)}, bf16[256,576]{1,0:T(8,128)(2,1)S(1)}, u32[]{:S(2)}, u32[]{:S(2)}) collective-permute-start(bf16[256,576]{1,0:T(8,128)(2,1)S(1)} %get-tuple-element.615), channel_id=1, source_target_pairs={{32,0},{40,8},{48,16},{56,24},{64,32},{72,40},{80,48},{88,56},{96,... | collective-permute-start | bytes 884744 | tf_op jit(solution)/shard_map/ppermute | solution.py:17
  238.0 14.6 %copy-start.6 = (s32[128]{0:T(128)S(1)}, s32[128]{0:T(128)}, u32[]{:S(2)}) copy-start(s32[128]{0:T(128)} %param.15) | copy-start | bytes 1540
  238.0 28.6 %copy-start.5 = (bf16[2,128,4,576]{1,3,2,0:T(8,128)(2,1)S(1)}, bf16[2,128,4,576]{1,3,2,0:T(8,128)(2,1)}, u32[]{:S(2)}) copy-start(bf16[2,128,4,576]{1,3,2,0:T(8,128)(2,1)} %get-tuple-element.440) | copy-start | bytes 3538948
  239.4 27.2 %collective-permute-start.4 = (bf16[128,4,576]{0,2,1:T(8,128)(2,1)S(1)}, bf16[128,4,576]{0,2,1:T(8,128)(2,1)S(1)}, u32[]{:S(2)}, u32[]{:S(2)}) collective-permute-start(bf16[128,4,576]{0,2,1:T(8,128)(2,1)S(1)} %get-tuple-element.619), channel_id=1, source_target_pairs={{0,256},{8,264},{16,272},{24,280},{32,288},{40,296},{48,304},{56,3... | collective-permute-start | bytes 1769480 | tf_op jit(solution)/shard_map/ppermute | solution.py:22
Sparse Core Ops, SparseCore 0:
  238.1 121.2 reduce-scatter.1
where the time goes:
time: 370 us; the launch traced here: 366 us
  waiting for transfers between devices  230 us (62%)
  local copies, waits for them, and re-layouts  48.3 us (13%)
  starting transfers between devices  33.4 us (9%)
  matrix products  20.9 us (6%)
  other arithmetic  15.1 us (4%)
  between operations  14.9 us (4%)
    ppermute x8, waiting for transfers between devices, from_behind(): return lax.ppermute(value, axis, pairs)  126 us
    reduce_scatter x1, waiting for transfers between devices, on_device(): lax.psum_scatter(gathered, 'head', scatter_dimension=0, tiled=True)  91.6 us
    ppermute x8, starting transfers between devices, from_behind(): return lax.ppermute(value, axis, pairs)  20.3 us
    ppermute x1, starting transfers between devices, passed_along(): lax.ppermute(value, axis, [(i, (i + by) % peers) for i in range(peers)])  13.1 us
    ppermute x1, waiting for transfers between devices, passed_along(): lax.ppermute(value, axis, [(i, (i + by) % peers) for i in range(peers)])  12.7 us
    another operation x13, local copies, waits for them, and re-layouts  9.1 us
  transfers between devices with their start and end apart: 10, of which 8 were waited for; matrix products, arithmetic and copies ran while one was open for 2% of the time, Pallas kernels for 0%

commit v1 on v0

v1 whole, which is shorter than its diff:
```python
import functools

import jax
import jax.numpy as jnp
from jax import lax
from jax.experimental import pallas as pl
from jax.experimental.pallas import tpu as pltpu
from jax.sharding import PartitionSpec as P

BLOCK = 128
SCORE_SCALE = 192.0 ** (-0.5)
MASKED_FILL = -1e30
MESH = pl.DeviceIdType.MESH

HEADS_DEV = 4
TOK = 256
ROWS = TOK * HEADS_DEV
QK = 576
LAT = 512
WIDE = 640
BACK = 4
WIN = (BACK + 1) * TOK
CHUNK = 256
TILE = 128
PIECE = 32
HALF = TOK // 2

NT = (((1,), (1,)), ((), ()))


def mm(a, b):
    return jnp.dot(a, b, preferred_element_type=jnp.float32)


def mm_nt(a, b):
    return lax.dot_general(a, b, NT, preferred_element_type=jnp.float32)


def fused(
    q_hbm, k_hbm, g_hbm, len_ref,
    dq0_out, own_out, got_out, lat_out,
    q_in, k_in, g_in, q_all, g_all, win, win_t, scores, vgrads, probs, sgrads,
    top, start_of, pos_of, grads, dq0, dq1,
    r1_out, r1_in, r2_out, r2_in, r3_out, r3_in, r4_out, r4_in, lat,
    in_sem, out_sem, s1, v1, s2, v2, s3, v3, st, vt, sr1, vr1, sr2, vr2, sr3, vr3, sr4, vr4,
):
    ctx = lax.axis_index("ctx")
    head = lax.axis_index("head")
    n_ctx = lax.axis_size("ctx")
    n_y = 4
    y = head // 2
    core = head % 2
    x = ctx % 4
    zbase = ctx - x

    def at_ctx(by):
        return {"ctx": lax.rem(ctx + by + n_ctx, n_ctx)}

    def at_y(by):
        return {"head": lax.rem(y + by, n_y) * 2 + core}

    sibling = {"head": y * 2 + (1 - core)}

    peers = [at_ctx(b) for b in (1, 2, 3, 4, -1, -2, -3, -4, n_ctx // 2)]
    peers += [at_y(b) for b in (1, 2, 3)] + [sibling]
    barrier = pltpu.get_barrier_semaphore()
    for peer in peers:
        pl.semaphore_signal(barrier, inc=1, device_id=peer, device_id_type=MESH)

    load_k = pltpu.make_async_copy(k_hbm, k_in, in_sem.at[0])
    load_q = pltpu.make_async_copy(q_hbm, q_in, in_sem.at[1])
    load_g = pltpu.make_async_copy(g_hbm, g_in, in_sem.at[2])
    load_k.start()
    load_q.start()
    load_g.start()
    load_k.wait()

    own0 = BACK * TOK
    keys = jnp.transpose(k_in[...])
    win[pl.ds(own0, TOK), QK:] = jnp.zeros((TOK, WIDE - QK), jnp.bfloat16)
    for c in range(2):
        for yy in range(4):
            at = own0 + c * HALF + yy * PIECE
            frm = yy * 2 * PIECE + c * PIECE
            win[at:at + PIECE, :QK] = keys[frm:frm + PIECE, :]

    mine = core * HALF + y * PIECE
    pl.semaphore_wait(barrier, len(peers))

    def piece(slot):
        return win.at[pl.ds(pl.multiple_of(slot * TOK + mine, PIECE), PIECE), :]

    def half(slot):
        return win.at[pl.ds(pl.multiple_of(slot * TOK + core * HALF, HALF), HALF), :]

    def remote(src, dst, ss, rs, to):
        return pltpu.make_async_remote_copy(
            src_ref=src, dst_ref=dst, send_sem=ss, recv_sem=rs, device_id=to, device_id_type=MESH
        )

    hops = (4, 1, 3, 2)
    first = [remote(piece(BACK), piece(BACK - d), s1.at[d - 1], v1.at[d - 1], at_ctx(d)) for d in hops]
    for copy in first:
        copy.start()

    load_q.wait()
    q_all[QK:, :] = jnp.zeros((WIDE - QK, ROWS), jnp.bfloat16)
    for b in range(2):
        for h in range(HEADS_DEV):
            at = b * 512 + h * BLOCK
            q_all[:QK, at:at + BLOCK] = q_in[h, :, b * BLOCK:(b + 1) * BLOCK]

    lane = lax.broadcasted_iota(jnp.int32, (1, ROWS), 1)
    q_pos = ctx * TOK + (lane // 512) * BLOCK + lane % BLOCK
    begin = jnp.zeros((1, ROWS), jnp.int32)
    total = jnp.int32(0)
    for d in range(len_ref.shape[0]):
        begin = jnp.where(q_pos >= total, total, begin)
        total = total + len_ref[d]
    pos_of[...] = q_pos
    start_of[...] = begin
    top[...] = jnp.full(top.shape, MASKED_FILL, jnp.float32)

    load_g.wait()
    to_row = lax.broadcasted_iota(jnp.int32, (CHUNK, CHUNK), 0)
    from_row = lax.broadcasted_iota(jnp.int32, (CHUNK, CHUNK), 1)
    shuffle = (from_row == (to_row % 64) * HEADS_DEV + to_row // 64).astype(jnp.bfloat16)
    for k in range(4):
        rows = g_in[k * 64:(k + 1) * 64].reshape(CHUNK, LAT)
        rows = mm(shuffle, rows).astype(jnp.bfloat16)
        for h in range(HEADS_DEV):
            at = (k // 2) * 512 + h * BLOCK + (k % 2) * 64
            g_all[at:at + 64, :] = rows[h * 64:(h + 1) * 64, :]

    def tile_scores(slot):
        at = slot * TOK
        keys = win[at:at + TOK, :]
        win_t[:, at:at + TOK] = jnp.transpose(keys)
        row = lax.broadcasted_iota(jnp.int32, (TOK, CHUNK), 0)
        k_pos = (ctx - BACK + slot) * TOK + ((row % HALF) // PIECE) * 2 * PIECE + (row // HALF) * PIECE + row % PIECE

        def chunk(n, _):
            lanes = pl.ds(pl.multiple_of(n * CHUNK, CHUNK), CHUNK)
            s = mm(keys, q_all[:, lanes]) * SCORE_SCALE
            allowed = (k_pos >= start_of[:, lanes]) & (k_pos <= pos_of[:, lanes])
            s = jnp.where(allowed, s, MASKED_FILL)
            scores[at:at + TOK, lanes] = s
            top[:, lanes] = jnp.maximum(top[:, lanes], jnp.max(s.reshape(TOK // 8, 8, CHUNK), axis=0))
            vgrads[at:at + TOK, lanes] = mm_nt(keys[:, :LAT], g_all[lanes, :])
            return 0

        lax.fori_loop(0, ROWS // CHUNK, chunk, 0)

    second = {}
    for i, d in enumerate(hops):
        first[i].wait_recv()
        second[d] = [
            remote(piece(BACK - d), piece(BACK - d), s2.at[d - 1, b - 1], v2.at[d - 1, b - 1], at_y(b)) for b in (1, 3, 2)
        ]
        for copy in second[d]:
            copy.start()

    tile_scores(BACK)
    third = []
    for d in hops:
        for copy in second[d]:
            copy.wait_recv()
        copy = remote(half(BACK - d), half(BACK - d), s3.at[d - 1], v3.at[d - 1], sibling)
        copy.start()
        third.append(copy)
    for i, d in enumerate(hops):
        third[i].wait_recv()
        tile_scores(BACK - d)

    def query_chunk(n, dq):
        lanes = slice(n * CHUNK, (n + 1) * CHUNK)
        peak = jnp.max(top[:, lanes], axis=0, keepdims=True)

        def weigh(i, carry):
            denom, mix = carry
            rows = pl.ds(pl.multiple_of(i * TILE, TILE), TILE)
            p = jnp.exp(scores[rows, lanes] - peak)
            scores[rows, lanes] = p
            pd = p * vgrads[rows, lanes]
            denom = denom + jnp.sum(p.reshape(TILE // 8, 8, CHUNK), axis=0)
            mix = mix + jnp.sum(pd.reshape(TILE // 8, 8, CHUNK), axis=0)
            return denom, mix

        zero = jnp.zeros((8, CHUNK), jnp.float32)
        denom, mix = lax.fori_loop(0, WIN // TILE, weigh, (zero, zero))
        inv = 1.0 / jnp.sum(denom, axis=0, keepdims=True)
        delta = jnp.sum(mix, axis=0, keepdims=True) * inv

        def finish(i, _):
            rows = pl.ds(pl.multiple_of(i * TILE, TILE), TILE)
            p = scores[rows, lanes] * inv
            probs[rows, lanes] = p.astype(jnp.bfloat16)
            sgrads[rows, lanes] = (p * (vgrads[rows, lanes] - delta)).astype(jnp.bfloat16)
            return 0

        lax.fori_loop(0, WIN // TILE, finish, 0)
        out, h = dq
        grad = (mm(win_t[:QK, :], sgrads[:, lanes]) * SCORE_SCALE).astype(jnp.bfloat16)
        out[h] = grad[:, :BLOCK]
        out[h + 1] = grad[:, BLOCK:]

    trade = []
    for n in (2, 3):
        h = (n - 2) * 2
        query_chunk(n, (dq1, h))
        for k in (h, h + 1):
            copy = remote(dq1.at[k], got_out.at[k], st.at[k], vt.at[k], at_ctx(n_ctx // 2))
            copy.start()
            trade.append(copy)
    keep_own = pltpu.make_async_copy(dq1, own_out, out_sem.at[0])
    keep_own.start()
    query_chunk(0, (dq0, 0))
    query_chunk(1, (dq0, 2))
    keep_first = pltpu.make_async_copy(dq0, dq0_out, out_sem.at[1])
    keep_first.start()

    def key_grads(slot, _):
        rows = pl.ds(pl.multiple_of(slot * TOK, TOK), TOK)
        grads[rows, :] = mm_nt(sgrads[rows, :], q_all[...]) * SCORE_SCALE
        grads[rows, :LAT] += mm(probs[rows, :], g_all[...])
        theirs = pl.ds(pl.multiple_of(slot * TOK + (1 - core) * HALF, HALF), HALF)
        r1_out[pl.ds(pl.multiple_of(slot * HALF, HALF), HALF), :] = grads[theirs, :].astype(jnp.bfloat16)
        return 0

    lax.fori_loop(0, BACK + 1, key_grads, 0)
    swap = remote(r1_out, r1_in, sr1, vr1, sibling)
    swap.start()
    swap.wait_recv()

    for slot in range(BACK + 1):
        ours = pl.ds(pl.multiple_of(slot * TOK + core * HALF, HALF), HALF)
        grads[ours, :] += r1_in[slot * HALF:(slot + 1) * HALF, :].astype(jnp.float32)
    spread = []
    for b in (1, 3, 2):
        to = lax.rem(y + b, n_y)
        for slot in range(BACK + 1):
            rows = pl.ds(pl.multiple_of(slot * TOK + core * HALF + to * PIECE, PIECE), PIECE)
            r2_out[b - 1, slot * PIECE:(slot + 1) * PIECE, :] = grads[rows, :].astype(jnp.bfloat16)
        copy = remote(r2_out.at[b - 1], r2_in.at[b - 1], sr2.at[b - 1], vr2.at[b - 1], at_y(b))
        copy.start()
        spread.append(copy)
    for copy in spread:
        copy.wait_recv()
    sums = []
    for slot in range(BACK + 1):
        rows = pl.ds(pl.multiple_of(slot * TOK + mine, PIECE), PIECE)
        part = grads[rows, :]
        for b in range(3):
            part = part + r2_in[b, slot * PIECE:(slot + 1) * PIECE, :].astype(jnp.float32)
        sums.append(part)

    along = []
    for d in (1, 3, 2):
        r3_out[d - 1] = sums[BACK - d].astype(jnp.bfloat16)
        to = {"ctx": zbase + lax.rem(x - d + 4, 4)}
        copy = remote(r3_out.at[d - 1], r3_in.at[d - 1], sr3.at[d - 1], vr3.at[d - 1], to)
        copy.start()
        along.append(copy)
    for copy in along:
        copy.wait_recv()
    here = sums[BACK]
    before = sums[0]
    for d in (1, 2, 3):
        part = r3_in[d - 1].astype(jnp.float32)
        inside = x + d < 4
        here = here + jnp.where(inside, part, 0.0)
        before = before + jnp.where(inside, 0.0, part)
    r4_out[...] = before.astype(jnp.bfloat16)
    down = remote(r4_out, r4_in, sr4, vr4, at_ctx(-4))
    down.start()
    down.wait_recv()
    lat[...] = (here + r4_in[...].astype(jnp.float32))[:, :QK]
    keep_lat = pltpu.make_async_copy(lat, lat_out, out_sem.at[2])
    keep_lat.start()

    for copy in first + [c for d in hops for c in second[d]] + third + [swap] + spread + along + [down]:
        copy.wait_send()
    keep_own.wait()
    keep_first.wait()
    keep_lat.wait()
    for copy in trade:
        copy.wait_send()
    for copy in trade:
        copy.wait_recv()


def on_device(queries, latent_kv, out_grad, lengths, block_plan):
    bf16, f32, i32 = jnp.bfloat16, jnp.float32, jnp.int32
    any_space = pl.BlockSpec(memory_space=pl.ANY)
    dma = pltpu.SemaphoreType.DMA
    block_shape = (HEADS_DEV, QK, BLOCK)
    vmem = pltpu.VMEM
    first, own, got, latent_grad = pl.pallas_call(
        fused,
        out_shape=[jax.ShapeDtypeStruct(block_shape, bf16)] * 3 + [jax.ShapeDtypeStruct((PIECE, QK), f32)],
        in_specs=[any_space] * 3 + [pl.BlockSpec(memory_space=pltpu.SMEM)],
        out_specs=[any_space] * 4,
        scratch_shapes=[
            vmem((HEADS_DEV, QK, TOK), bf16),
            vmem((QK, TOK), bf16),
            vmem((TOK, HEADS_DEV, LAT), bf16),
            vmem((WIDE, ROWS), bf16),
            vmem((ROWS, LAT), bf16),
            vmem((WIN, WIDE), bf16),
            vmem((WIDE, WIN), bf16),
            vmem((WIN, ROWS), f32),
            vmem((WIN, ROWS), f32),
            vmem((WIN, ROWS), bf16),
            vmem((WIN, ROWS), bf16),
            vmem((8, ROWS), f32),
            vmem((1, ROWS), i32),
            vmem((1, ROWS), i32),
            vmem((WIN, WIDE), f32),
            vmem(block_shape, bf16),
            vmem(block_shape, bf16),
            vmem(((BACK + 1) * HALF, WIDE), bf16),
            vmem(((BACK + 1) * HALF, WIDE), bf16),
            vmem((3, (BACK + 1) * PIECE, WIDE), bf16),
            vmem((3, (BACK + 1) * PIECE, WIDE), bf16),
            vmem((3, PIECE, WIDE), bf16),
            vmem((3, PIECE, WIDE), bf16),
            vmem((PIECE, WIDE), bf16),
            vmem((PIECE, WIDE), bf16),
            vmem((PIECE, QK), f32),
            dma((3,)), dma((3,)),
            dma((4,)), dma((4,)), dma((4, 3)), dma((4, 3)), dma((4,)), dma((4,)),
            dma((4,)), dma((4,)),
            dma, dma, dma((3,)), dma((3,)), dma((3,)), dma((3,)), dma, dma,
        ],
        compiler_params=pltpu.CompilerParams(
            collective_id=0, has_side_effects=True, vmem_limit_bytes=48 * 1024 * 1024
        ),
        cost_estimate=pl.CostEstimate(flops=8_000_000_000, bytes_accessed=8_000_000, transcendentals=1_300_000),
    )(jnp.transpose(queries, (1, 2, 0)), jnp.transpose(latent_kv), out_grad, lengths)

    position = lax.axis_index("ctx")
    blocks_here = TOK // BLOCK
    last_block = position * blocks_here + blocks_here - 1
    holder = jnp.sum(jnp.where(jnp.arange(block_plan.shape[0], dtype=i32) == last_block, block_plan, 0))
    last = jnp.where(holder != position, got, own)
    query_grad = jnp.transpose(jnp.concatenate([first, last], axis=2), (2, 0, 1))
    return query_grad, latent_grad


def solution(mesh):
    return jax.shard_map(
        on_device,
        mesh=mesh,
        in_specs=(P("ctx", "head", None), P("ctx", None), P("ctx", "head", None), P(), P()),
        out_specs=(P("ctx", "head", None), P(("ctx", "head"), None)),
        check_vma=False,
    )
```

time: 370 us -> 101 us (0.27)
  waiting for transfers between devices: 230 us -> 0 us
  Pallas kernels: 0 us -> 92.1 us
  local copies, waits for them, and re-layouts: 48.3 us -> 4.74 us
  starting transfers between devices: 33.4 us -> 0 us
  matrix products: 20.9 us -> 0 us
  between operations: 14.9 us -> 1.32 us
  other arithmetic: 15.1 us -> 2.51 us
    ppermute x9 -> x0, waiting for transfers between devices: 138 us -> none  [the longest x8 126 us: from_behind(): return lax.ppermute(value, axis, pairs)]
    pallas_call x0 -> x1, Pallas kernels: none -> 92.1 us  [on_device(): pl.pallas_call(fused, out_shape=[jax.ShapeDtypeStruct(block_shape, bf16)]...]
    reduce_scatter x1 -> x0, waiting for transfers between devices: 91.6 us -> none  [on_device(): lax.psum_scatter(gathered, 'head', scatter_dimension=0, tiled=True)]
    ppermute x9 -> x0, starting transfers between devices: 33.4 us -> none  [the longest x8 20.3 us: from_behind(): return lax.ppermute(value, axis, pairs)]
    dot_general x15 -> x0, matrix products: 20.9 us -> none  [the longest x3 7.07 us: second_pass(): jnp.einsum('rk,rc->kc', score_grad, query_rows, preferred_element_type=jn...]
    dynamic_slice x9 -> x0, local copies, waits for them, and re-layouts: 9.47 us -> none  [the longest x6 6.26 us: local_blocks(): return lax.scan(advance, jnp.zeros(window.shape, jnp.float32), inputs)]
    another operation x13 -> x0, local copies, waits for them, and re-layouts: 9.1 us -> none
    convert_element_type x4 -> x0, local copies, waits for them, and re-layouts: 7.05 us -> none  [advance(): return (window_grad + window_part, query_grad.astype(jnp.bfloat16))]
  transfers between devices with their start and end apart: 10 -> 0, of which waited for: 8 -> 0; matrix products, arithmetic and copies ran while one was open for 2% -> 0% of each run, Pallas kernels for 0% -> 0%
where the time goes in v1:
time: 101 us
  Pallas kernels  92.1 us (91%)
  local copies, waits for them, and re-layouts  4.74 us (5%)
  other arithmetic  2.51 us (2%)
  between operations  1.32 us (1%)
    pallas_call x1, Pallas kernels, on_device(): pl.pallas_call(fused, out_shape=[jax.ShapeDtypeStruct(block_shape, bf16)]...  92.1 us
    unnamed x9, local copies, waits for them, and re-layouts  4.74 us

profile of v1, /device:TPU:1, one launch (start us, length us, event | category | flops | bytes accessed | tf_op | source)
XLA Modules:
  0.0 100.7 jit_solution(17257790863297446019)
XLA Ops:
  0.6 1.3 %fusion = s32[]{:T(128)} fusion(s32[128]{0:T(128)} %param.9, s32[]{:T(128)S(6)} %sub.3), kind=kLoop, calls=%fused_computation.3 | loop fusion | flops 383 | bytes 520 | tf_op jit(solution)/shard_map/reduce_sum | solution.py:344
  2.6 0.0 copy-start
  2.6 1.3 %copy-done = bf16[256,4,576]{0,2,1:T(8,128)(2,1)S(1)} copy-done((bf16[256,4,576]{0,2,1:T(8,128)(2,1)S(1)}, bf16[256,4,576]{0,2,1:T(8,128)(2,1)}, u32[]{:S(2)}) %copy-start) | copy-done | bytes 1179672
  3.9 0.0 copy-start.1
  3.9 1.2 %copy-done.1 = bf16[256,4,512]{2,1,0:T(4,128)(2,1)S(1)} copy-done((bf16[256,4,512]{2,1,0:T(4,128)(2,1)S(1)}, bf16[256,4,512]{2,1,0:T(4,128)(2,1)}, u32[]{:S(2)}) %copy-start.1) | copy-done | bytes 1048600
  5.1 0.0 copy-start.2
  5.1 1.0 copy-done.2
  6.0 0.0 copy-start.3
  6.0 0.7 copy-done.3
  6.7 92.1 %shard_map.68 = (bf16[4,576,128]{2,1,0:T(8,128)(2,1)S(1)}, bf16[4,576,128]{2,1,0:T(8,128)(2,1)S(1)}, bf16[4,576,128]{2,1,0:T(8,128)(2,1)S(1)}, f32[32,576]{1,0:T(8,128)S(1)}) custom-call(bf16[4,576,256]{2,1,0:T(8,128)(2,1)S(1)} %bitcast.4, bf16[576,256]{1,0:T(8,128)(2,1)S(1)} %bitcast.5, bf16[256,4,512]{2,1,0:T(4,128)(2,1)S(1)} %copy-done.1, s32[32]{0:T(128)S(1)} %copy-done.3), custom_call_target="tpu_custom_call" | custom-call | flops 8000000000 | bytes 8000000 | tf_op jit(solution)/shard_map/pallas_call | solution.py:298
  98.9 0.1 broadcast_select_fusion
  98.9 1.1 %maximum_bitcast_fusion = bf16[256,4,576]{0,2,1:T(8,128)(2,1)} fusion(bf16[4,576,128]{2,1,0:T(8,128)(2,1)S(1)} %broadcast_select_fusion, bf16[4,576,128]{2,1,0:T(8,128)(2,1)S(1)} %get-tuple-element.6), kind=kLoop, calls=%fused_computation | loop fusion | flops 2359296 | bytes 2359296 | tf_op jit(solution)/shard_map/transpose | solution.py:346
  100.1 0.6 copy.8
Async XLA Ops:
  2.6 1.3 %copy-start = (bf16[256,4,576]{0,2,1:T(8,128)(2,1)S(1)}, bf16[256,4,576]{0,2,1:T(8,128)(2,1)}, u32[]{:S(2)}) copy-start(bf16[256,4,576]{0,2,1:T(8,128)(2,1)} %param.5) | copy-start | bytes 3538948
  3.9 1.2 %copy-start.1 = (bf16[256,4,512]{2,1,0:T(4,128)(2,1)S(1)}, bf16[256,4,512]{2,1,0:T(4,128)(2,1)}, u32[]{:S(2)}) copy-start(bf16[256,4,512]{2,1,0:T(4,128)(2,1)} %g_hbm.1) | copy-start | bytes 3145732
  5.1 1.0 copy-start.2
  6.0 0.7 copy-start.3

commit v2 on v1

--- a/solution.py
+++ b/solution.py
@@ -24,6 +24,8 @@
 TILE = 128
 PIECE = 32
 HALF = TOK // 2
+FAR = 16
+VMEM_BYTES = 63 * 1024 * 1024
 
 NT = (((1,), (1,)), ((), ()))
 
@@ -37,12 +39,12 @@
 
 
 def fused(
-    q_hbm, k_hbm, g_hbm, len_ref,
-    dq0_out, own_out, got_out, lat_out,
+    q_hbm, k_hbm, g_hbm, len_ref, plan_ref,
+    dq_out, lat_out,
     q_in, k_in, g_in, q_all, g_all, win, win_t, scores, vgrads, probs, sgrads,
-    top, start_of, pos_of, grads, dq0, dq1,
+    top, start_of, pos_of, grads, dq0, dq1, mid, got,
     r1_out, r1_in, r2_out, r2_in, r3_out, r3_in, r4_out, r4_in, lat,
-    in_sem, out_sem, s1, v1, s2, v2, s3, v3, st, vt, sr1, vr1, sr2, vr2, sr3, vr3, sr4, vr4,
+    in_sem, out_sem, s1, v1, s2, v2, s3, v3, st, vt, su, vu, sr1, vr1, sr2, vr2, sr3, vr3, sr4, vr4,
 ):
     ctx = lax.axis_index("ctx")
     head = lax.axis_index("head")
@@ -61,18 +63,17 @@
 
     sibling = {"head": y * 2 + (1 - core)}
 
-    peers = [at_ctx(b) for b in (1, 2, 3, 4, -1, -2, -3, -4, n_ctx // 2)]
+    peers = [at_ctx(b) for b in (1, 2, 3, 4, -1, -2, -3, -4, FAR, -FAR)]
     peers += [at_y(b) for b in (1, 2, 3)] + [sibling]
-    barrier = pltpu.get_barrier_semaphore()
-    for peer in peers:
-        pl.semaphore_signal(barrier, inc=1, device_id=peer, device_id_type=MESH)
-
     load_k = pltpu.make_async_copy(k_hbm, k_in, in_sem.at[0])
     load_q = pltpu.make_async_copy(q_hbm, q_in, in_sem.at[1])
     load_g = pltpu.make_async_copy(g_hbm, g_in, in_sem.at[2])
     load_k.start()
     load_q.start()
     load_g.start()
+    barrier = pltpu.get_barrier_semaphore()
+    for peer in peers:
+        pl.semaphore_signal(barrier, inc=1, device_id=peer, device_id_type=MESH)
     load_k.wait()
 
     own0 = BACK * TOK
@@ -87,8 +88,9 @@
     mine = core * HALF + y * PIECE
     pl.semaphore_wait(barrier, len(peers))
 
-    def piece(slot):
-        return win.at[pl.ds(pl.multiple_of(slot * TOK + mine, PIECE), PIECE), :]
+    def piece(slot, by=0, first=0, size=PIECE):
+        at = slot * TOK + core * HALF + lax.rem(y + by, n_y) * PIECE + first
+        return win.at[pl.ds(pl.multiple_of(at, 16), size), :]
 
     def half(slot):
         return win.at[pl.ds(pl.multiple_of(slot * TOK + core * HALF, HALF), HALF), :]
@@ -121,59 +123,74 @@
     start_of[...] = begin
     top[...] = jnp.full(top.shape, MASKED_FILL, jnp.float32)
 
+    def tile_scores(slot, lane0, count, width, turn=False):
+        rows = pl.ds(pl.multiple_of(slot * TOK, TOK), TOK)
+        keys = win[rows, :]
+        if turn:
+            win_t[:, rows] = jnp.transpose(keys)
+        row = lax.broadcasted_iota(jnp.int32, (TOK, width), 0)
+        k_pos = (ctx - BACK + slot) * TOK + ((row % HALF) // PIECE) * 2 * PIECE + (row // HALF) * PIECE + row % PIECE
+
+        def chunk(n, _):
+            lanes = pl.ds(pl.multiple_of(lane0 + n * width, width), width)
+            s = mm(keys, q_all[:, lanes]) * SCORE_SCALE
+            allowed = (k_pos >= start_of[:, lanes]) & (k_pos <= pos_of[:, lanes])
+            s = jnp.where(allowed, s, MASKED_FILL)
+            scores[rows, lanes] = s
+            top[:, lanes] = jnp.maximum(top[:, lanes], jnp.max(s.reshape(TOK // 8, 8, width), axis=0))
+            vgrads[rows, lanes] = mm_nt(keys[:, :LAT], g_all[lanes, :])
+            return 0
+
+        if count == 1:
+            chunk(0, 0)
+        else:
+            lax.fori_loop(0, count, chunk, 0)
+
+    def earlier_scores(lane0, width):
+        def step(slot, _):
+            tile_scores(slot, lane0, 1, width)
+            return 0
+
+        lax.fori_loop(0, BACK, step, 0)
+
+    second, third = {}, {}
+    for d in hops:
+        slot = BACK - d
+        first[hops.index(d)].wait_recv()
+        second[d] = [
+            remote(piece(slot), piece(slot), s2.at[d - 1, b - 1], v2.at[d - 1, b - 1], at_y(b)) for b in (1, 3, 2)
+        ]
+        for copy in second[d]:
+            copy.start()
+
     load_g.wait()
     to_row = lax.broadcasted_iota(jnp.int32, (CHUNK, CHUNK), 0)
     from_row = lax.broadcasted_iota(jnp.int32, (CHUNK, CHUNK), 1)
     shuffle = (from_row == (to_row % 64) * HEADS_DEV + to_row // 64).astype(jnp.bfloat16)
-    for k in range(4):
+
+    def shuffle_rows(k):
         rows = g_in[k * 64:(k + 1) * 64].reshape(CHUNK, LAT)
         rows = mm(shuffle, rows).astype(jnp.bfloat16)
         for h in range(HEADS_DEV):
             at = (k // 2) * 512 + h * BLOCK + (k % 2) * 64
             g_all[at:at + 64, :] = rows[h * 64:(h + 1) * 64, :]
 
-    def tile_scores(slot):
-        at = slot * TOK
-        keys = win[at:at + TOK, :]
-        win_t[:, at:at + TOK] = jnp.transpose(keys)
-        row = lax.broadcasted_iota(jnp.int32, (TOK, CHUNK), 0)
-        k_pos = (ctx - BACK + slot) * TOK + ((row % HALF) // PIECE) * 2 * PIECE + (row // HALF) * PIECE + row % PIECE
-
-        def chunk(n, _):
-            lanes = pl.ds(pl.multiple_of(n * CHUNK, CHUNK), CHUNK)
-            s = mm(keys, q_all[:, lanes]) * SCORE_SCALE
-            allowed = (k_pos >= start_of[:, lanes]) & (k_pos <= pos_of[:, lanes])
-            s = jnp.where(allowed, s, MASKED_FILL)
-            scores[at:at + TOK, lanes] = s
-            top[:, lanes] = jnp.maximum(top[:, lanes], jnp.max(s.reshape(TOK // 8, 8, CHUNK), axis=0))
-            vgrads[at:at + TOK, lanes] = mm_nt(keys[:, :LAT], g_all[lanes, :])
-            return 0
-
-        lax.fori_loop(0, ROWS // CHUNK, chunk, 0)
-
-    second = {}
+    for k in range(4):
+        shuffle_rows(k)
+    tile_scores(BACK, 512, 4, BLOCK, True)
     for i, d in enumerate(hops):
-        first[i].wait_recv()
-        second[d] = [
-            remote(piece(BACK - d), piece(BACK - d), s2.at[d - 1, b - 1], v2.at[d - 1, b - 1], at_y(b)) for b in (1, 3, 2)
-        ]
-        for copy in second[d]:
-            copy.start()
-
-    tile_scores(BACK)
-    third = []
-    for d in hops:
         for copy in second[d]:
             copy.wait_recv()
-        copy = remote(half(BACK - d), half(BACK - d), s3.at[d - 1], v3.at[d - 1], sibling)
-        copy.start()
-        third.append(copy)
-    for i, d in enumerate(hops):
-        third[i].wait_recv()
-        tile_scores(BACK - d)
-
-    def query_chunk(n, dq):
-        lanes = slice(n * CHUNK, (n + 1) * CHUNK)
+        third[d] = remote(half(BACK - d), half(BACK - d), s3.at[d - 1], v3.at[d - 1], sibling)
+        third[d].start()
+        if i == 1:
+            tile_scores(BACK, 0, 2, CHUNK)
+    for d in hops:
+        third[d].wait_recv()
+        tile_scores(BACK - d, 512, 1, BLOCK, True)
+
+    def query_chunk(lane0, width, out, h):
+        lanes = slice(lane0, lane0 + width)
         peak = jnp.max(top[:, lanes], axis=0, keepdims=True)
 
         def weigh(i, carry):
@@ -182,11 +199,11 @@
             p = jnp.exp(scores[rows, lanes] - peak)
             scores[rows, lanes] = p
             pd = p * vgrads[rows, lanes]
-            denom = denom + jnp.sum(p.reshape(TILE // 8, 8, CHUNK), axis=0)
-            mix = mix + jnp.sum(pd.reshape(TILE // 8, 8, CHUNK), axis=0)
+            denom = denom + jnp.sum(p.reshape(TILE // 8, 8, width), axis=0)
+            mix = mix + jnp.sum(pd.reshape(TILE // 8, 8, width), axis=0)
             return denom, mix
 
-        zero = jnp.zeros((8, CHUNK), jnp.float32)
+        zero = jnp.zeros((8, width), jnp.float32)
         denom, mix = lax.fori_loop(0, WIN // TILE, weigh, (zero, zero))
         inv = 1.0 / jnp.sum(denom, axis=0, keepdims=True)
         delta = jnp.sum(mix, axis=0, keepdims=True) * inv
@@ -199,25 +216,34 @@
             return 0
 
         lax.fori_loop(0, WIN // TILE, finish, 0)
-        out, h = dq
         grad = (mm(win_t[:QK, :], sgrads[:, lanes]) * SCORE_SCALE).astype(jnp.bfloat16)
-        out[h] = grad[:, :BLOCK]
-        out[h + 1] = grad[:, BLOCK:]
-
+        for k in range(width // BLOCK):
+            out[h + k] = grad[:, k * BLOCK:(k + 1) * BLOCK]
+
+    ways = ((slice(0, QK // 2), FAR), (slice(QK // 2, QK), -FAR))
     trade = []
-    for n in (2, 3):
-        h = (n - 2) * 2
-        query_chunk(n, (dq1, h))
-        for k in (h, h + 1):
-            copy = remote(dq1.at[k], got_out.at[k], st.at[k], vt.at[k], at_ctx(n_ctx // 2))
+    for k in range(HEADS_DEV):
+        if k > 0:
+            earlier_scores(512 + k * BLOCK, BLOCK)
+        query_chunk(512 + k * BLOCK, BLOCK, dq1, k)
+        for w, (rows, by) in enumerate(ways):
+            copy = remote(dq1.at[k, rows], mid.at[k, rows], st.at[k, w], vt.at[k, w], at_ctx(by))
             copy.start()
             trade.append(copy)
-    keep_own = pltpu.make_async_copy(dq1, own_out, out_sem.at[0])
-    keep_own.start()
-    query_chunk(0, (dq0, 0))
-    query_chunk(1, (dq0, 2))
-    keep_first = pltpu.make_async_copy(dq0, dq0_out, out_sem.at[1])
-    keep_first.start()
+    onward = []
+
+    def pass_on(k):
+        for w, (rows, by) in enumerate(ways):
+            trade[2 * k + w].wait_recv()
+            copy = remote(mid.at[k, rows], got.at[k, rows], su.at[k, w], vu.at[k, w], at_ctx(by))
+            copy.start()
+            onward.append(copy)
+
+    for n in range(2):
+        earlier_scores(n * CHUNK, CHUNK)
+        query_chunk(n * CHUNK, CHUNK, dq0, 2 * n)
+    keep = [pltpu.make_async_copy(dq0, dq_out.at[:, :, :BLOCK], out_sem.at[0])]
+    keep[0].start()
 
     def key_grads(slot, _):
         rows = pl.ds(pl.multiple_of(slot * TOK, TOK), TOK)
@@ -230,6 +256,7 @@
     lax.fori_loop(0, BACK + 1, key_grads, 0)
     swap = remote(r1_out, r1_in, sr1, vr1, sibling)
     swap.start()
+    pass_on(0)
     swap.wait_recv()
 
     for slot in range(BACK + 1):
@@ -244,6 +271,7 @@
         copy = remote(r2_out.at[b - 1], r2_in.at[b - 1], sr2.at[b - 1], vr2.at[b - 1], at_y(b))
         copy.start()
         spread.append(copy)
+    pass_on(1)
     for copy in spread:
         copy.wait_recv()
     sums = []
@@ -261,6 +289,7 @@
         copy = remote(r3_out.at[d - 1], r3_in.at[d - 1], sr3.at[d - 1], vr3.at[d - 1], to)
         copy.start()
         along.append(copy)
+    pass_on(2)
     for copy in along:
         copy.wait_recv()
     here = sums[BACK]
@@ -273,33 +302,52 @@
     r4_out[...] = before.astype(jnp.bfloat16)
     down = remote(r4_out, r4_in, sr4, vr4, at_ctx(-4))
     down.start()
+    pass_on(3)
     down.wait_recv()
     lat[...] = (here + r4_in[...].astype(jnp.float32))[:, :QK]
-    keep_lat = pltpu.make_async_copy(lat, lat_out, out_sem.at[2])
-    keep_lat.start()
-
-    for copy in first + [c for d in hops for c in second[d]] + third + [swap] + spread + along + [down]:
+    keep.append(pltpu.make_async_copy(lat, lat_out, out_sem.at[1]))
+    keep[1].start()
+    sent = first + [c for d in hops for c in second[d] + [third[d]]]
+    for copy in sent + [swap] + spread + along + [down] + trade:
         copy.wait_send()
-    keep_own.wait()
-    keep_first.wait()
-    keep_lat.wait()
-    for copy in trade:
+    traded = plan_ref[2 * ctx + 1] != ctx
+    for k in range(HEADS_DEV):
+        for copy in onward[2 * k:2 * k + 2]:
+            copy.wait_recv()
+        dq1[k] = jnp.where(traded, got[k], dq1[k])
+        keep.append(pltpu.make_async_copy(dq1.at[k], dq_out.at[k, :, BLOCK:], out_sem.at[2 + k]))
+        keep[-1].start()
+    for copy in onward:
         copy.wait_send()
-    for copy in trade:
-        copy.wait_recv()
+    for copy in keep:
+        copy.wait()
+
+
+def place(dq_in, lat_in, dq_out, lat_out, dq_held, lat_held, in_sem, out_sem):
+    parts = [(dq_in.at[h], dq_held.at[h], dq_out.at[h]) for h in range(HEADS_DEV)] + [(lat_in, lat_held, lat_out)]
+    loads = [pltpu.make_async_copy(src, held, in_sem.at[i]) for i, (src, held, _) in enumerate(parts)]
+    stores = [pltpu.make_async_copy(held, dst, out_sem.at[i]) for i, (_, held, dst) in enumerate(parts)]
+    for load in loads:
+        load.start()
+    for load, store in zip(loads, stores):
+        load.wait()
+        store.start()
+    for store in stores:
+        store.wait()
 
 
 def on_device(queries, latent_kv, out_grad, lengths, block_plan):
     bf16, f32, i32 = jnp.bfloat16, jnp.float32, jnp.int32
-    any_space = pl.BlockSpec(memory_space=pl.ANY)
+    hbm = pl.BlockSpec(memory_space=pl.ANY)
+    smem = pl.BlockSpec(memory_space=pltpu.SMEM)
     dma = pltpu.SemaphoreType.DMA
     block_shape = (HEADS_DEV, QK, BLOCK)
     vmem = pltpu.VMEM
-    first, own, got, latent_grad = pl.pallas_call(
+    query_grad, latent_grad = pl.pallas_call(
         fused,
-        out_shape=[jax.ShapeDtypeStruct(block_shape, bf16)] * 3 + [jax.ShapeDtypeStruct((PIECE, QK), f32)],
-        in_specs=[any_space] * 3 + [pl.BlockSpec(memory_space=pltpu.SMEM)],
-        out_specs=[any_space] * 4,
+        out_shape=[jax.ShapeDtypeStruct((HEADS_DEV, QK, TOK), bf16), jax.ShapeDtypeStruct((PIECE, QK), f32)],
+        in_specs=[hbm] * 3 + [smem] * 2,
+        out_specs=[hbm] * 2,
         scratch_shapes=[
             vmem((HEADS_DEV, QK, TOK), bf16),
             vmem((QK, TOK), bf16),
@@ -318,6 +366,8 @@
             vmem((WIN, WIDE), f32),
             vmem(block_shape, bf16),
             vmem(block_shape, bf16),
+            vmem(block_shape, bf16),
+            vmem(block_shape, bf16),
             vmem(((BACK + 1) * HALF, WIDE), bf16),
             vmem(((BACK + 1) * HALF, WIDE), bf16),
             vmem((3, (BACK + 1) * PIECE, WIDE), bf16),
@@ -327,24 +377,28 @@
             vmem((PIECE, WIDE), bf16),
             vmem((PIECE, WIDE), bf16),
             vmem((PIECE, QK), f32),
-            dma((3,)), dma((3,)),
+            dma((3,)), dma((6,)),
             dma((4,)), dma((4,)), dma((4, 3)), dma((4, 3)), dma((4,)), dma((4,)),
-            dma((4,)), dma((4,)),
+            dma((4, 2)), dma((4, 2)), dma((4, 2)), dma((4, 2)),
             dma, dma, dma((3,)), dma((3,)), dma((3,)), dma((3,)), dma, dma,
         ],
         compiler_params=pltpu.CompilerParams(
-            collective_id=0, has_side_effects=True, vmem_limit_bytes=48 * 1024 * 1024
+            collective_id=0, has_side_effects=True, vmem_limit_bytes=VMEM_BYTES
         ),
         cost_estimate=pl.CostEstimate(flops=8_000_000_000, bytes_accessed=8_000_000, transcendentals=1_300_000),
-    )(jnp.transpose(queries, (1, 2, 0)), jnp.transpose(latent_kv), out_grad, lengths)
-
-    position = lax.axis_index("ctx")
-    blocks_here = TOK // BLOCK
-    last_block = position * blocks_here + blocks_here - 1
-    holder = jnp.sum(jnp.where(jnp.arange(block_plan.shape[0], dtype=i32) == last_block, block_plan, 0))
-    last = jnp.where(holder != position, got, own)
-    query_grad = jnp.transpose(jnp.concatenate([first, last], axis=2), (2, 0, 1))
-    return query_grad, latent_grad
+    )(jnp.transpose(queries, (1, 2, 0)), jnp.transpose(latent_kv), out_grad, lengths, block_plan)
+
+    query_grad, latent_grad = pl.pallas_call(
+        place,
+        out_shape=[jax.ShapeDtypeStruct(query_grad.shape, bf16), jax.ShapeDtypeStruct(latent_grad.shape, f32)],
+        in_specs=[hbm] * 2,
+        out_specs=[hbm] * 2,
+        scratch_shapes=[
+            vmem(query_grad.shape, bf16), vmem(latent_grad.shape, f32), dma((HEADS_DEV + 1,)), dma((HEADS_DEV + 1,)),
+        ],
+        compiler_params=pltpu.CompilerParams(vmem_limit_bytes=VMEM_BYTES),
+    )(query_grad, latent_grad)
+    return jnp.transpose(query_grad, (2, 0, 1)), latent_grad
 
 
 def solution(mesh):

time: 101 us -> 92.7 us (0.918)
  local copies, waits for them, and re-layouts: 4.74 us -> 0 us
  other arithmetic: 2.51 us -> 0 us
    unnamed x9 -> x0, local copies, waits for them, and re-layouts: 4.74 us -> none
    reduce_sum x1 -> x0, other arithmetic: 1.29 us -> none  [on_device(): jnp.sum(jnp.where(jnp.arange(block_plan.shape[0], dtype=i32) == last_bloc...]
    transpose x1 -> x0, other arithmetic: 1.15 us -> none  [on_device(): jnp.transpose(jnp.concatenate([first, last], axis=2), (2, 0, 1))]
    pallas_call x1 -> x2, Pallas kernels: 92.1 us -> 91.9 us  [the longest x1 89.9 us: on_device(): pl.pallas_call(fused, out_shape=[jax.ShapeDtypeStruct((HEADS_DEV, QK, TOK...]
where the time goes in v2:
time: 92.7 us; the launch traced here: 92.6 us
  Pallas kernels  91.9 us (99%)
    pallas_call x1, Pallas kernels, on_device(): pl.pallas_call(fused, out_shape=[jax.ShapeDtypeStruct((HEADS_DEV, QK, TOK...  89.9 us
    pallas_call x1, Pallas kernels, on_device(): pl.pallas_call(place, out_shape=[jax.ShapeDtypeStruct(query_grad.shape, b...  2.07 us

profile of v2, /device:TPU:1, one launch (start us, length us, event | category | flops | bytes accessed | tf_op | source)
XLA Modules:
  0.0 92.6 jit_solution(3880607329768225172)
XLA Ops:
  0.6 89.9 %shard_map.68 = (bf16[4,576,256]{2,1,0:T(8,128)(2,1)}, f32[32,576]{1,0:T(8,128)}) custom-call(bf16[4,576,256]{2,1,0:T(8,128)(2,1)} %bitcast.3, bf16[576,256]{1,0:T(8,128)(2,1)} %bitcast.5, bf16[256,4,512]{2,1,0:T(4,128)(2,1)} %g_hbm.1, s32[32]{0:T(128)} %len_ref.1, s32[128]{0:T(128)} %plan_ref.1), custom_call_target="tpu_custom_call" | custom-call | flops 8000000000 | bytes 8000000 | tf_op jit(solution)/shard_map/pallas_call | solution.py:346
  90.5 2.1 %shard_map.69 = (bf16[4,576,256]{2,1,0:T(8,128)(2,1)}, f32[32,576]{1,0:T(8,128)}) custom-call(bf16[4,576,256]{2,1,0:T(8,128)(2,1)} %get-tuple-element.6.dq_in, f32[32,576]{1,0:T(8,128)} %get-tuple-element.7.lat_in), custom_call_target="tpu_custom_call" | custom-call | tf_op jit(solution)/shard_map/pallas_call | solution.py:391

commit v3 on v2

--- a/solution.py
+++ b/solution.py
@@ -22,6 +22,7 @@
 WIN = (BACK + 1) * TOK
 CHUNK = 256
 TILE = 128
+STRIP = QK // 4
 PIECE = 32
 HALF = TOK // 2
 FAR = 16
@@ -41,10 +42,10 @@
 def fused(
     q_hbm, k_hbm, g_hbm, len_ref, plan_ref,
     dq_out, lat_out,
-    q_in, k_in, g_in, q_all, g_all, win, win_t, scores, vgrads, probs, sgrads,
+    q_in, g_in, q_all, g_all, win, win_t, scores, vgrads, probs, sgrads,
     top, start_of, pos_of, grads, dq0, dq1, mid, got,
     r1_out, r1_in, r2_out, r2_in, r3_out, r3_in, r4_out, r4_in, lat,
-    in_sem, out_sem, s1, v1, s2, v2, s3, v3, st, vt, su, vu, sr1, vr1, sr2, vr2, sr3, vr3, sr4, vr4,
+    in_sem, out_sem, s1, v1, sx, vx, s2, v2, s3, v3, st, vt, su, vu, sr1, vr1, sr2, vr2, sr3, vr3, sr4, vr4,
 ):
     ctx = lax.axis_index("ctx")
     head = lax.axis_index("head")
@@ -65,7 +66,8 @@
 
     peers = [at_ctx(b) for b in (1, 2, 3, 4, -1, -2, -3, -4, FAR, -FAR)]
     peers += [at_y(b) for b in (1, 2, 3)] + [sibling]
-    load_k = pltpu.make_async_copy(k_hbm, k_in, in_sem.at[0])
+    own_at = BACK * TOK
+    load_k = pltpu.make_async_copy(k_hbm, win_t.at[pl.ds(0, QK), pl.ds(own_at, TOK)], in_sem.at[0])
     load_q = pltpu.make_async_copy(q_hbm, q_in, in_sem.at[1])
     load_g = pltpu.make_async_copy(g_hbm, g_in, in_sem.at[2])
     load_k.start()
@@ -74,36 +76,27 @@
     barrier = pltpu.get_barrier_semaphore()
     for peer in peers:
         pl.semaphore_signal(barrier, inc=1, device_id=peer, device_id_type=MESH)
-    load_k.wait()
-
-    own0 = BACK * TOK
-    keys = jnp.transpose(k_in[...])
-    win[pl.ds(own0, TOK), QK:] = jnp.zeros((TOK, WIDE - QK), jnp.bfloat16)
-    for c in range(2):
-        for yy in range(4):
-            at = own0 + c * HALF + yy * PIECE
-            frm = yy * 2 * PIECE + c * PIECE
-            win[at:at + PIECE, :QK] = keys[frm:frm + PIECE, :]
-
-    mine = core * HALF + y * PIECE
+    win_t[QK:, :] = jnp.zeros((WIDE - QK, WIN), jnp.bfloat16)
     pl.semaphore_wait(barrier, len(peers))
-
-    def piece(slot, by=0, first=0, size=PIECE):
-        at = slot * TOK + core * HALF + lax.rem(y + by, n_y) * PIECE + first
-        return win.at[pl.ds(pl.multiple_of(at, 16), size), :]
+    keys_of_core = pl.ds(pl.multiple_of(core * HALF, HALF), HALF)
+    columns = pl.ds(pl.multiple_of(y * STRIP, 16), STRIP)
 
     def half(slot):
-        return win.at[pl.ds(pl.multiple_of(slot * TOK + core * HALF, HALF), HALF), :]
+        return win_t.at[pl.ds(0, QK), pl.ds(pl.multiple_of(slot * TOK + core * HALF, HALF), HALF)]
+
+    def piece(slot):
+        return win_t.at[columns, pl.ds(pl.multiple_of(slot * TOK + core * HALF, HALF), HALF)]
 
     def remote(src, dst, ss, rs, to):
         return pltpu.make_async_remote_copy(
             src_ref=src, dst_ref=dst, send_sem=ss, recv_sem=rs, device_id=to, device_id_type=MESH
         )
 
-    hops = (4, 1, 3, 2)
-    first = [remote(piece(BACK), piece(BACK - d), s1.at[d - 1], v1.at[d - 1], at_ctx(d)) for d in hops]
-    for copy in first:
-        copy.start()
+    hops = (1, 3, 2)
+    beside = {d: remote(k_hbm.at[columns, keys_of_core], piece(BACK - d), sx.at[d - 1], vx.at[d - 1], at_ctx(d)) for d in hops}
+    for d in hops:
+        beside[d].start()
+    up = [remote(k_hbm.at[:, keys_of_core], half(0), s1, v1, at_ctx(BACK))]
 
     load_q.wait()
     q_all[QK:, :] = jnp.zeros((WIDE - QK, ROWS), jnp.bfloat16)
@@ -125,11 +118,13 @@
 
     def tile_scores(slot, lane0, count, width, turn=False):
         rows = pl.ds(pl.multiple_of(slot * TOK, TOK), TOK)
-        keys = win[rows, :]
         if turn:
-            win_t[:, rows] = jnp.transpose(keys)
+            keys = jnp.transpose(win_t[:, rows])
+            win[rows, :] = keys
+        else:
+            keys = win[rows, :]
         row = lax.broadcasted_iota(jnp.int32, (TOK, width), 0)
-        k_pos = (ctx - BACK + slot) * TOK + ((row % HALF) // PIECE) * 2 * PIECE + (row // HALF) * PIECE + row % PIECE
+        k_pos = (ctx - BACK + slot) * TOK + row
 
         def chunk(n, _):
             lanes = pl.ds(pl.multiple_of(lane0 + n * width, width), width)
@@ -156,12 +151,15 @@
     second, third = {}, {}
     for d in hops:
         slot = BACK - d
-        first[hops.index(d)].wait_recv()
+        beside[d].wait_recv()
         second[d] = [
             remote(piece(slot), piece(slot), s2.at[d - 1, b - 1], v2.at[d - 1, b - 1], at_y(b)) for b in (1, 3, 2)
         ]
         for copy in second[d]:
             copy.start()
+        if d == hops[0]:
+            for copy in up:
+                copy.start()
 
     load_g.wait()
     to_row = lax.broadcasted_iota(jnp.int32, (CHUNK, CHUNK), 0)
@@ -177,17 +175,23 @@
 
     for k in range(4):
         shuffle_rows(k)
+    load_k.wait()
     tile_scores(BACK, 512, 4, BLOCK, True)
-    for i, d in enumerate(hops):
+    def exchange(slot):
+        third[slot] = remote(half(slot), half(slot), s3.at[slot], v3.at[slot], sibling)
+        third[slot].start()
+
+    for d in hops:
         for copy in second[d]:
             copy.wait_recv()
-        third[d] = remote(half(BACK - d), half(BACK - d), s3.at[d - 1], v3.at[d - 1], sibling)
-        third[d].start()
-        if i == 1:
-            tile_scores(BACK, 0, 2, CHUNK)
-    for d in hops:
-        third[d].wait_recv()
-        tile_scores(BACK - d, 512, 1, BLOCK, True)
+        exchange(BACK - d)
+        if d == hops[0]:
+            for copy in up:
+                copy.wait_recv()
+            exchange(0)
+    for slot in (BACK - hops[0], 0, BACK - hops[1], BACK - hops[2]):
+        third[slot].wait_recv()
+        tile_scores(slot, 512, 1, BLOCK, True)
 
     def query_chunk(lane0, width, out, h):
         lanes = slice(lane0, lane0 + width)
@@ -240,17 +244,22 @@
             onward.append(copy)
 
     for n in range(2):
+        tile_scores(BACK, n * CHUNK, 1, CHUNK)
         earlier_scores(n * CHUNK, CHUNK)
         query_chunk(n * CHUNK, CHUNK, dq0, 2 * n)
     keep = [pltpu.make_async_copy(dq0, dq_out.at[:, :, :BLOCK], out_sem.at[0])]
     keep[0].start()
 
+    def owned(slot, of_y, of_core):
+        return pl.ds(pl.multiple_of(slot * TOK + of_y * 2 * PIECE + of_core * PIECE, PIECE), PIECE)
+
     def key_grads(slot, _):
         rows = pl.ds(pl.multiple_of(slot * TOK, TOK), TOK)
         grads[rows, :] = mm_nt(sgrads[rows, :], q_all[...]) * SCORE_SCALE
         grads[rows, :LAT] += mm(probs[rows, :], g_all[...])
-        theirs = pl.ds(pl.multiple_of(slot * TOK + (1 - core) * HALF, HALF), HALF)
-        r1_out[pl.ds(pl.multiple_of(slot * HALF, HALF), HALF), :] = grads[theirs, :].astype(jnp.bfloat16)
+        for yy in range(n_y):
+            held = pl.ds(pl.multiple_of(slot * HALF + yy * PIECE, PIECE), PIECE)
+            r1_out[held, :] = grads[owned(slot, yy, 1 - core), :].astype(jnp.bfloat16)
         return 0
 
     lax.fori_loop(0, BACK + 1, key_grads, 0)
@@ -259,15 +268,18 @@
     pass_on(0)
     swap.wait_recv()
 
-    for slot in range(BACK + 1):
-        ours = pl.ds(pl.multiple_of(slot * TOK + core * HALF, HALF), HALF)
-        grads[ours, :] += r1_in[slot * HALF:(slot + 1) * HALF, :].astype(jnp.float32)
+    def join(slot, _):
+        for yy in range(n_y):
+            held = pl.ds(pl.multiple_of(slot * HALF + yy * PIECE, PIECE), PIECE)
+            grads[owned(slot, yy, core), :] += r1_in[held, :].astype(jnp.float32)
+        return 0
+
+    lax.fori_loop(0, BACK + 1, join, 0)
     spread = []
     for b in (1, 3, 2):
         to = lax.rem(y + b, n_y)
         for slot in range(BACK + 1):
-            rows = pl.ds(pl.multiple_of(slot * TOK + core * HALF + to * PIECE, PIECE), PIECE)
-            r2_out[b - 1, slot * PIECE:(slot + 1) * PIECE, :] = grads[rows, :].astype(jnp.bfloat16)
+            r2_out[b - 1, slot * PIECE:(slot + 1) * PIECE, :] = grads[owned(slot, to, core), :].astype(jnp.bfloat16)
         copy = remote(r2_out.at[b - 1], r2_in.at[b - 1], sr2.at[b - 1], vr2.at[b - 1], at_y(b))
         copy.start()
         spread.append(copy)
@@ -276,8 +288,7 @@
         copy.wait_recv()
     sums = []
     for slot in range(BACK + 1):
-        rows = pl.ds(pl.multiple_of(slot * TOK + mine, PIECE), PIECE)
-        part = grads[rows, :]
+        part = grads[owned(slot, y, core), :]
         for b in range(3):
             part = part + r2_in[b, slot * PIECE:(slot + 1) * PIECE, :].astype(jnp.float32)
         sums.append(part)
@@ -307,7 +318,7 @@
     lat[...] = (here + r4_in[...].astype(jnp.float32))[:, :QK]
     keep.append(pltpu.make_async_copy(lat, lat_out, out_sem.at[1]))
     keep[1].start()
-    sent = first + [c for d in hops for c in second[d] + [third[d]]]
+    sent = up + [c for d in hops for c in second[d] + [beside[d]]] + [third[slot] for slot in range(BACK)]
     for copy in sent + [swap] + spread + along + [down] + trade:
         copy.wait_send()
     traded = plan_ref[2 * ctx + 1] != ctx
@@ -350,7 +361,6 @@
         out_specs=[hbm] * 2,
         scratch_shapes=[
             vmem((HEADS_DEV, QK, TOK), bf16),
-            vmem((QK, TOK), bf16),
             vmem((TOK, HEADS_DEV, LAT), bf16),
             vmem((WIDE, ROWS), bf16),
             vmem((ROWS, LAT), bf16),
@@ -378,7 +388,7 @@
             vmem((PIECE, WIDE), bf16),
             vmem((PIECE, QK), f32),
             dma((3,)), dma((6,)),
-            dma((4,)), dma((4,)), dma((4, 3)), dma((4, 3)), dma((4,)), dma((4,)),
+            dma, dma, dma((3,)), dma((3,)), dma((3, 3)), dma((3, 3)), dma((4,)), dma((4,)),
             dma((4, 2)), dma((4, 2)), dma((4, 2)), dma((4, 2)),
             dma, dma, dma((3,)), dma((3,)), dma((3,)), dma((3,)), dma, dma,
         ],

time: 92.7 us -> 89.9 us (0.970)
  the two profiles are of different devices: /device:TPU:1 before, /device:TPU:3 now
where the time goes in v3:
time: 89.9 us; the launch traced here: 89.7 us
  Pallas kernels  89.1 us (99%)
    pallas_call x1, Pallas kernels, on_device(): pl.pallas_call(fused, out_shape=[jax.ShapeDtypeStruct((HEADS_DEV, QK, TOK...  87 us
    pallas_call x1, Pallas kernels, on_device(): pl.pallas_call(place, out_shape=[jax.ShapeDtypeStruct(query_grad.shape, b...  2.07 us

profile of v3, /device:TPU:3, one launch (start us, length us, event | category | flops | bytes accessed | tf_op | source)
XLA Modules:
  0.0 89.7 jit_solution(168336816379527392)
XLA Ops:
  0.6 87.0 %shard_map.68 = (bf16[4,576,256]{2,1,0:T(8,128)(2,1)}, f32[32,576]{1,0:T(8,128)}) custom-call(bf16[4,576,256]{2,1,0:T(8,128)(2,1)} %bitcast.3, bf16[576,256]{1,0:T(8,128)(2,1)} %bitcast.5, bf16[256,4,512]{2,1,0:T(4,128)(2,1)} %g_hbm.1, s32[32]{0:T(128)} %len_ref.1, s32[128]{0:T(128)} %plan_ref.1), custom_call_target="tpu_custom_call" | custom-call | flops 8000000000 | bytes 8000000 | tf_op jit(solution)/shard_map/pallas_call | solution.py:357
  87.6 2.1 %shard_map.69 = (bf16[4,576,256]{2,1,0:T(8,128)(2,1)}, f32[32,576]{1,0:T(8,128)}) custom-call(bf16[4,576,256]{2,1,0:T(8,128)(2,1)} %get-tuple-element.6.dq_in, f32[32,576]{1,0:T(8,128)} %get-tuple-element.7.lat_in), custom_call_target="tpu_custom_call" | custom-call | tf_op jit(solution)/shard_map/pallas_call | solution.py:401

commit v4 on v3

--- a/solution.py
+++ b/solution.py
@@ -195,31 +195,32 @@
 
     def query_chunk(lane0, width, out, h):
         lanes = slice(lane0, lane0 + width)
+        tile = TILE * CHUNK // width
         peak = jnp.max(top[:, lanes], axis=0, keepdims=True)
 
         def weigh(i, carry):
             denom, mix = carry
-            rows = pl.ds(pl.multiple_of(i * TILE, TILE), TILE)
+            rows = pl.ds(pl.multiple_of(i * tile, tile), tile)
             p = jnp.exp(scores[rows, lanes] - peak)
             scores[rows, lanes] = p
             pd = p * vgrads[rows, lanes]
-            denom = denom + jnp.sum(p.reshape(TILE // 8, 8, width), axis=0)
-            mix = mix + jnp.sum(pd.reshape(TILE // 8, 8, width), axis=0)
+            denom = denom + jnp.sum(p.reshape(tile // 8, 8, width), axis=0)
+            mix = mix + jnp.sum(pd.reshape(tile // 8, 8, width), axis=0)
             return denom, mix
 
         zero = jnp.zeros((8, width), jnp.float32)
-        denom, mix = lax.fori_loop(0, WIN // TILE, weigh, (zero, zero))
+        denom, mix = lax.fori_loop(0, WIN // tile, weigh, (zero, zero))
         inv = 1.0 / jnp.sum(denom, axis=0, keepdims=True)
         delta = jnp.sum(mix, axis=0, keepdims=True) * inv
 
         def finish(i, _):
-            rows = pl.ds(pl.multiple_of(i * TILE, TILE), TILE)
+            rows = pl.ds(pl.multiple_of(i * tile, tile), tile)
             p = scores[rows, lanes] * inv
             probs[rows, lanes] = p.astype(jnp.bfloat16)
             sgrads[rows, lanes] = (p * (vgrads[rows, lanes] - delta)).astype(jnp.bfloat16)
             return 0
 
-        lax.fori_loop(0, WIN // TILE, finish, 0)
+        lax.fori_loop(0, WIN // tile, finish, 0)
         grad = (mm(win_t[:QK, :], sgrads[:, lanes]) * SCORE_SCALE).astype(jnp.bfloat16)
         for k in range(width // BLOCK):
             out[h + k] = grad[:, k * BLOCK:(k + 1) * BLOCK]
@@ -265,7 +266,6 @@
     lax.fori_loop(0, BACK + 1, key_grads, 0)
     swap = remote(r1_out, r1_in, sr1, vr1, sibling)
     swap.start()
-    pass_on(0)
     swap.wait_recv()
 
     def join(slot, _):
@@ -283,6 +283,7 @@
         copy = remote(r2_out.at[b - 1], r2_in.at[b - 1], sr2.at[b - 1], vr2.at[b - 1], at_y(b))
         copy.start()
         spread.append(copy)
+    pass_on(0)
     pass_on(1)
     for copy in spread:
         copy.wait_recv()

time: 89.9 us -> 88.9 us (0.989)
  the two profiles are of different devices: /device:TPU:3 before, /device:TPU:25 now
where the time goes in v4:
time: 88.9 us; the launch traced here: 88.8 us
  Pallas kernels  88.1 us (99%)
    pallas_call x1, Pallas kernels, on_device(): pl.pallas_call(fused, out_shape=[jax.ShapeDtypeStruct((HEADS_DEV, QK, TOK...  86.1 us
    pallas_call x1, Pallas kernels, on_device(): pl.pallas_call(place, out_shape=[jax.ShapeDtypeStruct(query_grad.shape, b...  2.07 us

profile of v4, /device:TPU:25, one launch (start us, length us, event | category | flops | bytes accessed | tf_op | source)
XLA Modules:
  0.0 88.8 jit_solution(12214321777779042719)
XLA Ops:
  0.6 86.1 %shard_map.68 = (bf16[4,576,256]{2,1,0:T(8,128)(2,1)}, f32[32,576]{1,0:T(8,128)}) custom-call(bf16[4,576,256]{2,1,0:T(8,128)(2,1)} %bitcast.3, bf16[576,256]{1,0:T(8,128)(2,1)} %bitcast.5, bf16[256,4,512]{2,1,0:T(4,128)(2,1)} %g_hbm.1, s32[32]{0:T(128)} %len_ref.1, s32[128]{0:T(128)} %plan_ref.1), custom_call_target="tpu_custom_call" | custom-call | flops 8000000000 | bytes 8000000 | tf_op jit(solution)/shard_map/pallas_call | solution.py:358
  86.7 2.1 %shard_map.69 = (bf16[4,576,256]{2,1,0:T(8,128)(2,1)}, f32[32,576]{1,0:T(8,128)}) custom-call(bf16[4,576,256]{2,1,0:T(8,128)(2,1)} %get-tuple-element.6.dq_in, f32[32,576]{1,0:T(8,128)} %get-tuple-element.7.lat_in), custom_call_target="tpu_custom_call" | custom-call | tf_op jit(solution)/shard_map/pallas_call | solution.py:402

commit v5 on v4

--- a/solution.py
+++ b/solution.py
@@ -196,6 +196,7 @@
     def query_chunk(lane0, width, out, h):
         lanes = slice(lane0, lane0 + width)
         tile = TILE * CHUNK // width
+        leads = lane0 == ROWS // 2
         peak = jnp.max(top[:, lanes], axis=0, keepdims=True)
 
         def weigh(i, carry):
@@ -209,7 +210,7 @@
             return denom, mix
 
         zero = jnp.zeros((8, width), jnp.float32)
-        denom, mix = lax.fori_loop(0, WIN // tile, weigh, (zero, zero))
+        denom, mix = lax.fori_loop(0, WIN // tile, weigh, (zero, zero), unroll=leads)
         inv = 1.0 / jnp.sum(denom, axis=0, keepdims=True)
         delta = jnp.sum(mix, axis=0, keepdims=True) * inv
 
@@ -220,7 +221,7 @@
             sgrads[rows, lanes] = (p * (vgrads[rows, lanes] - delta)).astype(jnp.bfloat16)
             return 0
 
-        lax.fori_loop(0, WIN // tile, finish, 0)
+        lax.fori_loop(0, WIN // tile, finish, 0, unroll=leads)
         grad = (mm(win_t[:QK, :], sgrads[:, lanes]) * SCORE_SCALE).astype(jnp.bfloat16)
         for k in range(width // BLOCK):
             out[h + k] = grad[:, k * BLOCK:(k + 1) * BLOCK]

time: 88.9 us -> 88.8 us (level)
  no operation moved by 1% of the time
where the time goes in v5:
time: 88.8 us; the launch traced here: 88.7 us
  Pallas kernels  88 us (99%)
    pallas_call x1, Pallas kernels, on_device(): pl.pallas_call(fused, out_shape=[jax.ShapeDtypeStruct((HEADS_DEV, QK, TOK...  86 us
    pallas_call x1, Pallas kernels, on_device(): pl.pallas_call(place, out_shape=[jax.ShapeDtypeStruct(query_grad.shape, b...  2.07 us

profile of v5, /device:TPU:25, one launch (start us, length us, event | category | flops | bytes accessed | tf_op | source)
XLA Modules:
  0.0 88.7 jit_solution(5625316771116648043)
XLA Ops:
  0.6 86.0 %shard_map.68 = (bf16[4,576,256]{2,1,0:T(8,128)(2,1)}, f32[32,576]{1,0:T(8,128)}) custom-call(bf16[4,576,256]{2,1,0:T(8,128)(2,1)} %bitcast.3, bf16[576,256]{1,0:T(8,128)(2,1)} %bitcast.5, bf16[256,4,512]{2,1,0:T(4,128)(2,1)} %g_hbm.1, s32[32]{0:T(128)} %len_ref.1, s32[128]{0:T(128)} %plan_ref.1), custom_call_target="tpu_custom_call" | custom-call | flops 8000000000 | bytes 8000000 | tf_op jit(solution)/shard_map/pallas_call | solution.py:359
  86.6 2.1 %shard_map.69 = (bf16[4,576,256]{2,1,0:T(8,128)(2,1)}, f32[32,576]{1,0:T(8,128)}) custom-call(bf16[4,576,256]{2,1,0:T(8,128)(2,1)} %get-tuple-element.6.dq_in, f32[32,576]{1,0:T(8,128)} %get-tuple-element.7.lat_in), custom_call_target="tpu_custom_call" | custom-call | tf_op jit(solution)/shard_map/pallas_call | solution.py:403
